TPU v7x, 32 devices: a whole 2x2x4 slice. The times are simulated.
32 devices in a mesh: stn: 8 (over z, y), sec: 4 (over x, core).
Axes of the slice: x: 2, y: 2, z: 4, core: 2. Of those that a mesh axis runs over, the one named last changes fastest.
Arguments:
- voltages: bfloat16 [2, 1024, 569344], P(None, ('stn', 'sec')), may hold values from -6 to 6
- fir_taps: float32 [12, 4096], replicated, may hold values from -1.75 to 1.75
- cor_channels: int32 [32], replicated, may hold values from 0 to 4095, as said below
- beam_channels: int32 [32], replicated, may hold values from 1 to 4094, as said below
- cor_gain: float32 [32], replicated, as said below
- beam_gain: float32 [32], replicated, as said below
- beam_stations: int32 [16, 512], replicated, may hold values from 0 to 511
- beam_codes: int32 [16, 512], replicated, may hold values from 0 to 255
Outputs:
- visibilities: bfloat16 [32, 2, 1024, 1024], P(('stn', 'sec'))
- beams: bfloat16 [32, 16, 2, 256], P(('stn', 'sec'))
Inputs may be any that keep to these rules, and one draw needn't show every extreme that they name: cor_channels and beam_channels together are 64 distinct transform channels. None of beam_channels appears in cor_channels. `cor_gain`: positive. `beam_gain`: positive.
All inputs are finite; a program needn't handle non-finite values.
Results may differ from a plain program's by a relative error of at most 0.0085.
Values may be sent and summed in bfloat16 or wider, within the bound.
A program may use at most 320 MiB of HBM per device.

v0:
```python
import math

import jax
import jax.numpy as jnp
from jax import lax
from jax.sharding import PartitionSpec as P

STATIONS = 512


epsilon = 1e-05


def make_tables(channel_of, points):
    sample_index = jnp.arange(points, dtype=jnp.int32)
    phase_turns = channel_of[:, None] * sample_index[None, :] % points
    phase_angle = phase_turns.astype(jnp.float32) * (2.0 * math.pi / points)
    table_scale = 1.0 / math.sqrt(points)
    cos_table = (jnp.cos(phase_angle) * table_scale).astype(jnp.bfloat16)
    sin_table = (jnp.sin(phase_angle) * table_scale).astype(jnp.bfloat16)
    return (cos_table, sin_table)


def make_weights(beam_stations, beam_codes, stations):
    station_ids = jnp.arange(stations, dtype=jnp.int32)
    onehot = (beam_stations[:, :, None] == station_ids[None, None, :]).astype(jnp.float32)
    amplitude = (1 + beam_codes // 64).astype(jnp.float32)
    phase_angle = (beam_codes % 64).astype(jnp.float32) * (2.0 * math.pi / 64.0)
    weight_re = jnp.einsum("bk,bks->bs", amplitude * jnp.cos(phase_angle), onehot)
    weight_im = jnp.einsum("bk,bks->bs", amplitude * jnp.sin(phase_angle), onehot)
    return (weight_re.astype(jnp.bfloat16), weight_im.astype(jnp.bfloat16))


def polyphase(in_block, fir_taps, spectra):
    tap_count, points = fir_taps.shape
    framed = in_block.reshape(in_block.shape[0], in_block.shape[1], -1, points)
    summed = jnp.zeros((framed.shape[0], framed.shape[1], spectra, points), jnp.float32)
    for tap_index in range(tap_count):
        summed = summed + fir_taps[tap_index] * framed[
            :, :, tap_index : tap_index + spectra, :
        ].astype(jnp.float32)
    return summed.astype(jnp.bfloat16)


def contract(left_rows, right_rows):
    contract_dims = (((1,), (1,)), ((), ()))
    return lax.dot_general(left_rows, right_rows, contract_dims, preferred_element_type=jnp.float32)


def spectrum(filtered, cos_table, sin_table, slot_gain):
    inputs_here, spectra, points = (filtered.shape[1], filtered.shape[2], filtered.shape[3])
    real_rows = filtered[0].reshape(inputs_here * spectra, points)
    imag_rows = filtered[1].reshape(inputs_here * spectra, points)
    spec_re = contract(cos_table, real_rows) + contract(sin_table, imag_rows)
    spec_im = contract(cos_table, imag_rows) - contract(sin_table, real_rows)
    combined = jnp.concatenate(
        [spec_re.reshape(-1, inputs_here, spectra), spec_im.reshape(-1, inputs_here, spectra)],
        axis=2,
    )
    return (combined * slot_gain[:, None, None]).astype(jnp.bfloat16)


def form_beams(beam_data, weight_re, weight_im):
    spectra = beam_data.shape[2] // 2
    samples = beam_data.reshape(beam_data.shape[0], -1, 2, beam_data.shape[2])
    with_re = jnp.einsum("bs,jspt->jbpt", weight_re, samples, preferred_element_type=jnp.float32)
    with_im = jnp.einsum("bs,jspt->jbpt", weight_im, samples, preferred_element_type=jnp.float32)
    out_re = with_re[..., :spectra] - with_im[..., spectra:]
    out_im = with_re[..., spectra:] + with_im[..., :spectra]
    return jnp.concatenate([out_re, out_im], axis=3)


def per_device(
    voltages, fir_taps, cor_channels, beam_channels, cor_gain, beam_gain, beam_stations, beam_codes
):
    tap_count, points = fir_taps.shape
    stn_count = lax.axis_size("stn")
    sec_count = lax.axis_size("sec")
    device_count = stn_count * sec_count
    inputs_here = voltages.shape[1]
    spectra = voltages.shape[2] // points - tap_count + 1
    filtered = polyphase(voltages, fir_taps, spectra)
    channel_of = jnp.concatenate([cor_channels, beam_channels])
    slot_gain = jnp.concatenate([cor_gain, beam_gain])
    cos_table, sin_table = make_tables(channel_of, points)
    weight_re, weight_im = make_weights(beam_stations, beam_codes, STATIONS)
    spectra_all = spectrum(filtered, cos_table, sin_table, slot_gain)
    outgoing = spectra_all.reshape(2, stn_count, sec_count, 1, 1, inputs_here, 2 * spectra)
    turned = lax.all_to_all(
        lax.all_to_all(outgoing, "stn", split_axis=1, concat_axis=3, tiled=True),
        "sec",
        split_axis=2,
        concat_axis=4,
        tiled=True,
    )
    received = turned.reshape(2, device_count * inputs_here, 2 * spectra)
    cor_data = received[0]
    beam_data = received[1:2]
    swapped = jnp.concatenate([cor_data[:, spectra:], -cor_data[:, :spectra]], axis=1)
    vis_re = contract(cor_data, cor_data) / spectra
    vis_im = contract(swapped, cor_data) / spectra
    visibilities = jnp.stack([vis_re, vis_im])[None].astype(jnp.bfloat16)
    raw_beams = form_beams(beam_data, weight_re, weight_im)
    local_power = jnp.sum(raw_beams * raw_beams, axis=(0, 2, 3))
    summed_power = lax.psum(local_power, ("stn", "sec"))
    beam_power = summed_power / (device_count * raw_beams.shape[2] * raw_beams.shape[3])
    beams = (raw_beams * lax.rsqrt(beam_power + epsilon)[None, :, None, None]).astype(jnp.bfloat16)
    return (visibilities, beams)


def solution(mesh):
    in_specs = (P(None, ("stn", "sec"), None), P(), P(), P(), P(), P(), P(), P())
    out_specs = (P(("stn", "sec"), None, None, None), P(("stn", "sec"), None, None, None))
    return jax.shard_map(
        per_device, mesh=mesh, in_specs=in_specs, out_specs=out_specs, check_vma=False
    )
```

profile of v0, /device:TPU:15, one launch (start us, length us, event | category | flops | bytes accessed | tf_op | source)
XLA Modules:
  0.0 649.1 jit_solution(1242801091641112402)
XLA Ops:
  0.6 2.3 fusion.58
  2.9 92.1 %reshape.175 = bf16[2,32,139,4096]{3,2,1,0:T(8,128)(2,1)} reshape(bf16[2,32,569344]{2,1,0:T(8,128)(2,1)} %param.8) | data formatting | bytes 145752064 | tf_op jit(solution)/shard_map/reshape | solution.py:36
  95.0 340.8 %add_convert_fusion = bf16[2,32,128,4096]{3,2,1,0:T(8,128)(2,1)} fusion(bf16[2,32,139,4096]{3,2,1,0:T(8,128)(2,1)} %reshape.175, f32[4096]{0:T(1024)S(1)} %bitcast.99, f32[4096]{0:T(1024)S(1)} %bitcast.100, f32[4096]{0:T(1024)S(1)} %bitcast.90, f32[4096]{0:T(1024)S(1)} %bitcast.91, f32[4096]{0:T(1024)S(1)} %bitcast.92, f32[4096]{0:T(1024)S(1)} %bitcast.93, ...), kind=kLoop, calls=%fused_computation | loop fusion | flops 1207959552 | bytes 872611840 | tf_op jit(solution)/shard_map/convert_element_type | solution.py:42
  435.8 0.0 copy-start.4
  435.8 0.0 copy-start.5
  435.8 43.5 %fusion.55 = (bf16[1,32,128,4096]{3,2,1,0:T(8,128)(2,1)}, bf16[1,32,128,4096]{3,2,1,0:T(8,128)(2,1)}) fusion(bf16[2,32,128,4096]{3,2,1,0:T(8,128)(2,1)} %add_convert_fusion), kind=kLoop, calls=%fused_computation.89 | loop fusion | bytes 134217728 | tf_op jit(solution)/shard_map/slice | solution.py:52
  479.3 0.0 copy-done.4
  479.3 0.0 copy-done.5
  479.3 0.1 pad_add_fusion
  479.4 18.9 %fusion.19 = f32[64,4096]{1,0:T(8,128)S(1)} fusion(bf16[4096,4096]{1,0:T(8,128)(2,1)} %bitcast.78, s32[64]{0:T(128)S(1)} %pad_add_fusion), kind=kOutput, calls=%fused_computation.36 | convolution fusion | flops 2151677952 | bytes 34603264 | tf_op jit(solution)/shard_map/dot_general | solution.py:47
  498.3 0.0 copy-start.1
  498.3 0.0 copy-start.2
  498.3 0.0 copy-start
  498.3 0.0 copy-start.3
  498.4 18.7 %fusion.18 = f32[64,4096]{1,0:T(8,128)S(1)} fusion(bf16[4096,4096]{1,0:T(8,128)(2,1)} %bitcast.80, s32[64]{0:T(128)S(1)} %pad_add_fusion), kind=kOutput, calls=%fused_computation.35 | convolution fusion | flops 2151677952 | bytes 34603264 | tf_op jit(solution)/shard_map/dot_general | solution.py:47
  517.1 18.9 %fusion.7 = f32[8,8,32,128]{3,1,2,0:T(8,128)S(1)} fusion(f32[64,4096]{1,0:T(8,128)S(1)} %fusion.19, bf16[4096,4096]{1,0:T(8,128)(2,1)} %bitcast.81, s32[64]{0:T(128)S(1)} %pad_add_fusion), kind=kOutput, calls=%fused_computation.19 | convolution fusion | flops 2151940096 | bytes 35651840 | tf_op jit(solution)/shard_map/dot_general | solution.py:47
  536.0 0.2 copy.35
  536.2 19.1 %fusion.8 = f32[8,8,32,128]{3,1,2,0:T(8,128)S(1)} fusion(f32[64,4096]{1,0:T(8,128)S(1)} %fusion.18, bf16[4096,4096]{1,0:T(8,128)(2,1)} %bitcast.79, s32[64]{0:T(128)S(1)} %pad_add_fusion), kind=kOutput, calls=%fused_computation.20 | convolution fusion | flops 2151940096 | bytes 35651840 | tf_op jit(solution)/shard_map/dot_general | solution.py:47
  555.3 0.2 copy.36
  555.5 0.0 copy-done.1
  555.5 0.1 concatenate.59
  555.6 0.0 copy-done.2
  555.6 0.1 concatenate.60
  555.7 0.2 fusion.4
  555.9 28.2 %all_to_all.33 = bf16[2,8,4,1,1,32,256]{6,5,2,0,4,3,1:T(8,128)(2,1)S(1)} all-to-all(bf16[2,8,4,1,1,32,256]{6,5,2,0,4,3,1:T(8,128)(2,1)S(1)} %fusion.4), channel_id=1, replica_groups=mesh['stn'=8,'sec'=4] {'stn'}, dimensions={1} | all-to-all | bytes 2097152 | tf_op jit(solution)/shard_map/all_to_all | solution.py:90
  584.1 1.1 copy.25
  585.2 5.8 all-to-all-start.1
  590.9 0.0 copy-done
  590.9 0.2 multiply_bitcast_fusion.1
  591.1 0.0 copy-done.3
  591.1 3.2 fusion
  594.3 3.2 fusion.1
  597.5 5.9 all-to-all-done.1
  603.5 0.1 copy.57
  603.6 0.1 fusion.56
  603.7 0.2 reshape.176
  603.9 0.2 convolution_bitcast_fusion
  604.1 0.2 convolution_bitcast_fusion.1
  604.2 0.1 fusion.57
  604.3 0.1 multiply_reduce_fusion
  604.4 0.7 fusion.5
  605.2 40.0 %psum.7 = f32[16]{0:T(128)S(1)} all-reduce(f32[16]{0:T(128)S(1)} %multiply_reduce_fusion), channel_id=1, replica_groups=mesh['stn'=8,'sec'=4] {'stn','sec'}, use_global_device_ids=true, to_apply=%region_1.2 | all-reduce | flops 16 | bytes 128 | tf_op jit(solution)/shard_map/psum | solution.py:105
  645.2 0.1 multiply_convert_fusion.8
  645.3 0.6 copy.29
  645.9 0.7 fusion.6
  646.7 2.4 pad_maximum_fusion
  (4 shorter events, 0.0 us)
Async XLA Ops:
  435.8 43.5 %copy-start.4 = (s32[32]{0:T(128)S(1)}, s32[32]{0:T(128)}, u32[]{:S(2)}) copy-start(s32[32]{0:T(128)} %param.11) | copy-start | bytes 388
  435.8 43.5 %copy-start.5 = (s32[32]{0:T(128)S(1)}, s32[32]{0:T(128)}, u32[]{:S(2)}) copy-start(s32[32]{0:T(128)} %param.10) | copy-start | bytes 388
  498.3 57.2 %copy-start.1 = (f32[32]{0:T(128)S(1)}, f32[32]{0:T(128)}, u32[]{:S(2)}) copy-start(f32[32]{0:T(128)} %param.12) | copy-start | bytes 388
  498.3 57.3 %copy-start.2 = (f32[32]{0:T(128)S(1)}, f32[32]{0:T(128)}, u32[]{:S(2)}) copy-start(f32[32]{0:T(128)} %param.13) | copy-start | bytes 388
  498.3 92.6 %copy-start = (s32[16,512]{1,0:T(8,128)S(1)}, s32[16,512]{1,0:T(8,128)}, u32[]{:S(2)}) copy-start(s32[16,512]{1,0:T(8,128)} %param.15) | copy-start | bytes 98308
  498.3 92.7 %copy-start.3 = (s32[16,512]{1,0:T(8,128)S(1)}, s32[16,512]{1,0:T(8,128)}, u32[]{:S(2)}) copy-start(s32[16,512]{1,0:T(8,128)} %param.14) | copy-start | bytes 98308
  585.2 18.3 %all-to-all-start.1 = ((bf16[2,1,4,8,1,32,256]{6,5,3,0,4,1,2:T(8,128)(2,1)}), bf16[2,1,4,8,1,32,256]{6,5,3,0,4,1,2:T(8,128)(2,1)S(1)}, u32[]{:S(2)}, u32[]{:S(2)}) async-start(bf16[2,1,4,8,1,32,256]{6,5,3,0,4,1,2:T(8,128)(2,1)} %copy.25), calls=%async_computation.1 | async-start | bytes 2097152 | tf_op jit(solution)/shard_map/all_to_all | solution.py:89
where the time goes:
time: 653 us; the launch traced here: 649 us
  other arithmetic  344 us (53%)
  local copies, waits for them, and re-layouts  141 us (22%)
  matrix products  83.9 us (13%)
  blocking collectives  68.2 us (10%)
    convert_element_type x1, other arithmetic, polyphase(): return summed.astype(jnp.bfloat16)  341 us
    reshape x1, local copies, waits for them, and re-layouts, polyphase(): framed = in_block.reshape(in_block.shape[0], in_block.shape[1], -1, points)  92.1 us
    dot_general x6, matrix products, contract(): lax.dot_general(left_rows, right_rows, contract_dims, preferred_element_t...  77.1 us
    slice x1, local copies, waits for them, and re-layouts, spectrum(): real_rows = filtered[0].reshape(inputs_here * spectra, points)  43.5 us
    psum x1, blocking collectives, per_device(): summed_power = lax.psum(local_power, ('stn', 'sec'))  40 us
    all_to_all x1, blocking collectives, per_device(): lax.all_to_all(outgoing, 'stn', split_axis=1, concat_axis=3, tiled=True)  28.2 us
  transfers between devices with their start and end apart: 1, of which 1 were waited for; matrix products, arithmetic and copies ran while one was open for 1% of the time, Pallas kernels for 0%

commit v1 on v0

--- a/solution.py
+++ b/solution.py
@@ -1,8 +1,11 @@
+import functools
 import math
 
 import jax
 import jax.numpy as jnp
 from jax import lax
+from jax.experimental import pallas as pl
+from jax.experimental.pallas import tpu as pltpu
 from jax.sharding import PartitionSpec as P
 
 STATIONS = 512
@@ -70,7 +73,7 @@
     return jnp.concatenate([out_re, out_im], axis=3)
 
 
-def per_device(
+def plain_device(
     voltages, fir_taps, cor_channels, beam_channels, cor_gain, beam_gain, beam_stations, beam_codes
 ):
     tap_count, points = fir_taps.shape
@@ -108,6 +111,293 @@
     return (visibilities, beams)
 
 
+MESH = pl.DeviceIdType.MESH
+ROWS = 16
+CHUNK = 512
+STEP = 256
+
+
+def split_tables(channel_of, points):
+    coarse = 1 << (int(math.log2(points)) // 2)
+    index = jnp.arange(coarse, dtype=jnp.int32)
+    other = jnp.arange(points // coarse, dtype=jnp.int32)
+
+    def pair(turns):
+        angle = (turns % points).astype(jnp.float32) * (2.0 * math.pi / points)
+        return jnp.cos(angle), jnp.sin(angle)
+
+    high_cos, high_sin = pair(other[:, None] * coarse * channel_of[None, :])
+    low_cos, low_sin = pair(index[:, None] * channel_of[None, :])
+    high_cos, high_sin = high_cos[:, None, :], high_sin[:, None, :]
+    low_cos, low_sin = low_cos[None], low_sin[None]
+    scale = 1.0 / math.sqrt(points)
+    cosine = ((high_cos * low_cos - high_sin * low_sin) * scale).astype(jnp.bfloat16)
+    sine = ((high_sin * low_cos + high_cos * low_sin) * scale).astype(jnp.bfloat16)
+    cosine = cosine.reshape(points, -1)
+    sine = sine.reshape(points, -1)
+    return jnp.stack(
+        [jnp.concatenate([cosine, -sine], axis=1), jnp.concatenate([sine, cosine], axis=1)]
+    )
+
+
+def tree_sum(terms):
+    while len(terms) > 1:
+        paired = [terms[k] + terms[k + 1] for k in range(0, len(terms) - 1, 2)]
+        if len(terms) % 2:
+            paired.append(terms[-1])
+        terms = paired
+    return terms[0]
+
+
+def channelize_kernel(
+    points, tap_count, frames, groups, volt_ref, taps_ref, table_ref, gain_ref, out_ref,
+    held, filtered, total, sem,
+):
+    chunks = points // CHUNK
+    spectra = frames - tap_count + 1
+    slots = gain_ref.shape[1] // 2
+    group, chunk = pl.program_id(0), pl.program_id(1)
+    step = group * chunks + chunk
+
+    def fetch(which, slot):
+        rows = pl.ds(pl.multiple_of((which // chunks) * ROWS, ROWS), ROWS)
+        start = (which % chunks) * CHUNK
+
+        def one(frame, carry):
+            lanes = pl.ds(pl.multiple_of(frame * points + start, CHUNK), CHUNK)
+            pltpu.make_async_copy(
+                volt_ref.at[:, rows, lanes], held.at[slot, frame], sem.at[slot]
+            ).start()
+            return carry
+
+        lax.fori_loop(0, frames, one, 0)
+
+    slot = step % 2
+
+    @pl.when(step == 0)
+    def _():
+        fetch(step, 0)
+
+    @pl.when(step + 1 < groups * chunks)
+    def _():
+        fetch(step + 1, 1 - slot)
+
+    pltpu.make_async_copy(held.at[slot], held.at[slot], sem.at[slot]).wait()
+
+    @pl.when(chunk == 0)
+    def _():
+        total[...] = jnp.zeros_like(total)
+
+    def unit(index, carry):
+        part, piece = index // (CHUNK // STEP), index % (CHUNK // STEP)
+        for tile in range(STEP // 128):
+            here = pl.multiple_of(piece * STEP + tile * 128, 128)
+            lanes = pl.ds(here, 128)
+            point = pl.ds(pl.multiple_of(chunk * CHUNK + here, 128), 128)
+            taps = [taps_ref[t, :, point] for t in range(tap_count)]
+            window = [held[slot, t, part, :, lanes] for t in range(tap_count - 1)]
+            for s in range(spectra):
+                window.append(held[slot, s + tap_count - 1, part, :, lanes])
+                value = tree_sum([tap * frame for tap, frame in zip(taps, window)])
+                filtered[s * ROWS : (s + 1) * ROWS, tile * 128 : (tile + 1) * 128] = value
+                window = window[1:]
+        span = pl.ds(pl.multiple_of(chunk * CHUNK + piece * STEP, STEP), STEP)
+        total[...] += jnp.dot(
+            filtered[...], table_ref[part, span, :], preferred_element_type=jnp.float32
+        )
+        return carry
+
+    lax.fori_loop(0, 2 * (CHUNK // STEP), unit, 0)
+
+    @pl.when(chunk == chunks - 1)
+    def _():
+        for row in range(ROWS):
+            mine = total[pl.ds(row, spectra, stride=ROWS), :] * gain_ref[...]
+            turned = mine.T.astype(jnp.bfloat16)
+            at = row * 2 * spectra
+            out_ref[:, at : at + spectra] = turned[:slots]
+            out_ref[:, at + spectra : at + 2 * spectra] = turned[slots:]
+
+
+def channelize(voltages, fir_taps, table, slot_gain):
+    tap_count, points = fir_taps.shape
+    inputs_here = voltages.shape[1]
+    frames = voltages.shape[2] // points
+    spectra = frames - tap_count + 1
+    slots = slot_gain.shape[0]
+    groups = inputs_here // ROWS
+    taps = jnp.broadcast_to(fir_taps.astype(jnp.bfloat16)[:, None, :], (tap_count, ROWS, points))
+    gain = jnp.concatenate([slot_gain, slot_gain])[None, :]
+    whole = pl.BlockSpec(memory_space=pltpu.VMEM)
+    width = ROWS * 2 * spectra
+    return pl.pallas_call(
+        functools.partial(channelize_kernel, points, tap_count, frames, groups),
+        grid=(groups, points // CHUNK),
+        out_shape=jax.ShapeDtypeStruct((slots, inputs_here * 2 * spectra), jnp.bfloat16),
+        in_specs=[pl.BlockSpec(memory_space=pl.ANY), whole, whole, whole],
+        out_specs=pl.BlockSpec((slots, width), lambda group, chunk: (0, group)),
+        scratch_shapes=[
+            pltpu.VMEM((2, frames, 2, ROWS, CHUNK), jnp.bfloat16),
+            pltpu.VMEM((spectra * ROWS, STEP), jnp.bfloat16),
+            pltpu.VMEM((spectra * ROWS, 2 * slots), jnp.float32),
+            pltpu.SemaphoreType.DMA((2,)),
+        ],
+        compiler_params=pltpu.CompilerParams(
+            dimension_semantics=("arbitrary", "arbitrary"), vmem_limit_bytes=48 * 1024 * 1024
+        ),
+        name="channelize",
+    )(voltages, taps, table, gain)
+
+
+def place_of(index, sec_count):
+    return (index // sec_count, lax.rem(index, sec_count))
+
+
+def greet_all(me, count, sec_count):
+    barrier = pltpu.get_barrier_semaphore()
+
+    def greet(k, carry):
+        pl.semaphore_signal(
+            barrier, inc=1, device_id=place_of(lax.rem(me + k, count), sec_count),
+            device_id_type=MESH,
+        )
+        return carry
+
+    lax.fori_loop(1, count, greet, 0)
+    pl.semaphore_wait(barrier, count - 1)
+
+
+def exchange_kernel(count, sec_count, x_ref, y_ref, send_sem, recv_sem, own_sem):
+    me = lax.axis_index("stn") * sec_count + lax.axis_index("sec")
+    own = pltpu.make_async_copy(x_ref.at[:, me], y_ref.at[:, me], own_sem)
+    own.start()
+    greet_all(me, count, sec_count)
+
+    def copy(k):
+        to = lax.rem(me + k, count)
+        return pltpu.make_async_remote_copy(
+            src_ref=x_ref.at[:, to],
+            dst_ref=y_ref.at[:, me],
+            send_sem=send_sem.at[k],
+            recv_sem=recv_sem.at[k],
+            device_id=place_of(to, sec_count),
+            device_id_type=MESH,
+        )
+
+    def start(k, carry):
+        copy(k).start()
+        return carry
+
+    def finish(k, carry):
+        copy(k).wait()
+        return carry
+
+    lax.fori_loop(1, count, start, 0)
+    lax.fori_loop(1, count, finish, 0)
+    own.wait()
+
+
+def exchange(x, count, sec_count):
+    return pl.pallas_call(
+        functools.partial(exchange_kernel, count, sec_count),
+        out_shape=jax.ShapeDtypeStruct(x.shape, x.dtype),
+        in_specs=[pl.BlockSpec(memory_space=pl.ANY)],
+        out_specs=pl.BlockSpec(memory_space=pl.ANY),
+        scratch_shapes=[
+            pltpu.SemaphoreType.DMA((count,)),
+            pltpu.SemaphoreType.DMA((count,)),
+            pltpu.SemaphoreType.DMA,
+        ],
+        compiler_params=pltpu.CompilerParams(collective_id=0, has_side_effects=True),
+        name="exchange",
+    )(x)
+
+
+def power_kernel(count, sec_count, x_ref, y_ref, slots, send_sem, recv_sem):
+    me = lax.axis_index("stn") * sec_count + lax.axis_index("sec")
+    greet_all(me, count, sec_count)
+
+    def copy(k):
+        return pltpu.make_async_remote_copy(
+            src_ref=x_ref,
+            dst_ref=slots.at[k],
+            send_sem=send_sem.at[k],
+            recv_sem=recv_sem.at[k],
+            device_id=place_of(lax.rem(me + k, count), sec_count),
+            device_id_type=MESH,
+        )
+
+    def start(k, carry):
+        copy(k).start()
+        return carry
+
+    def finish(k, carry):
+        copy(k).wait()
+        return carry
+
+    lax.fori_loop(1, count, start, 0)
+    slots[0] = x_ref[...]
+    lax.fori_loop(1, count, finish, 0)
+    y_ref[...] = jnp.sum(slots[...], axis=0)
+
+
+def total_power(local_power, count, sec_count):
+    beams = local_power.shape[0]
+    x = jnp.broadcast_to(local_power[:, None], (beams, 128))
+    summed = pl.pallas_call(
+        functools.partial(power_kernel, count, sec_count),
+        out_shape=jax.ShapeDtypeStruct(x.shape, x.dtype),
+        in_specs=[pl.BlockSpec(memory_space=pltpu.VMEM)],
+        out_specs=pl.BlockSpec(memory_space=pltpu.VMEM),
+        scratch_shapes=[
+            pltpu.VMEM((count,) + x.shape, x.dtype),
+            pltpu.SemaphoreType.DMA((count,)),
+            pltpu.SemaphoreType.DMA((count,)),
+        ],
+        compiler_params=pltpu.CompilerParams(collective_id=1, has_side_effects=True),
+        name="power",
+    )(x)
+    return summed[:, 0]
+
+
+def per_device(
+    voltages, fir_taps, cor_channels, beam_channels, cor_gain, beam_gain, beam_stations, beam_codes
+):
+    tap_count, points = fir_taps.shape
+    sec_count = lax.axis_size("sec")
+    device_count = lax.axis_size("stn") * sec_count
+    inputs_here = voltages.shape[1]
+    frames = voltages.shape[2] // points
+    spectra = frames - tap_count + 1
+    slots = 2 * cor_channels.shape[0]
+    fits = inputs_here % ROWS == 0 and points % CHUNK == 0 and spectra % 128 == 0
+    if not fits or slots != 2 * device_count or slots % 16:
+        return plain_device(
+            voltages, fir_taps, cor_channels, beam_channels, cor_gain, beam_gain,
+            beam_stations, beam_codes,
+        )
+    channel_of = jnp.concatenate([cor_channels, beam_channels])
+    slot_gain = jnp.concatenate([cor_gain, beam_gain])
+    table = split_tables(channel_of, points)
+    weight_re, weight_im = make_weights(beam_stations, beam_codes, STATIONS)
+    outgoing = channelize(voltages, fir_taps, table, slot_gain)
+    outgoing = outgoing.reshape(2, device_count, inputs_here, 2 * spectra)
+    received = exchange(outgoing, device_count, sec_count)
+    received = received.reshape(2, device_count * inputs_here, 2 * spectra)
+    cor_data = received[0]
+    beam_data = received[1:2]
+    raw_beams = form_beams(beam_data, weight_re, weight_im)
+    local_power = jnp.sum(raw_beams * raw_beams, axis=(0, 2, 3))
+    summed_power = total_power(local_power, device_count, sec_count)
+    swapped = jnp.concatenate([cor_data[:, spectra:], -cor_data[:, :spectra]], axis=1)
+    vis_re = contract(cor_data, cor_data) / spectra
+    vis_im = contract(swapped, cor_data) / spectra
+    visibilities = jnp.stack([vis_re, vis_im])[None].astype(jnp.bfloat16)
+    beam_power = summed_power / (device_count * raw_beams.shape[2] * raw_beams.shape[3])
+    beams = (raw_beams * lax.rsqrt(beam_power + epsilon)[None, :, None, None]).astype(jnp.bfloat16)
+    return (visibilities, beams)
+
+
 def solution(mesh):
     in_specs = (P(None, ("stn", "sec"), None), P(), P(), P(), P(), P(), P(), P())
     out_specs = (P(("stn", "sec"), None, None, None), P(("stn", "sec"), None, None, None))

time: 653 us -> 288 us (0.44)
  other arithmetic: 344 us -> 8.49 us
  Pallas kernels: 0 us -> 265 us
  local copies, waits for them, and re-layouts: 141 us -> 4.18 us
  matrix products: 83.9 us -> 9.1 us
  blocking collectives: 68.2 us -> 0 us
    convert_element_type x2, other arithmetic: 341 us -> 0.7 us  [the longest x1 0.68 us: split_tables(): ((high_sin * low_cos + high_cos * low_sin) * scale).astype(jnp.bfloat16)]
    pallas_call x0 -> x3, Pallas kernels: none -> 265 us  [the longest x1 222 us: channelize(): pl.pallas_call(functools.partial(channelize_kernel, points, tap_count, fr...]
    reshape x1 -> x0, local copies, waits for them, and re-layouts: 92.1 us -> none  [polyphase(): framed = in_block.reshape(in_block.shape[0], in_block.shape[1], -1, points)]
    dot_general x6 -> x2, matrix products: 77.1 us -> 1.48 us  [contract(): lax.dot_general(left_rows, right_rows, contract_dims, preferred_element_t...]
    slice x2 -> x0, local copies, waits for them, and re-layouts: 45.7 us -> none  [the longest x1 43.5 us: spectrum(): real_rows = filtered[0].reshape(inputs_here * spectra, points)]
    psum x1 -> x0, blocking collectives: 40 us -> none  [per_device(): summed_power = lax.psum(local_power, ('stn', 'sec'))]
    all_to_all x1 -> x0, blocking collectives: 28.2 us -> none  [per_device(): lax.all_to_all(outgoing, 'stn', split_axis=1, concat_axis=3, tiled=True)]
  transfers between devices with their start and end apart: 1 -> 0, of which waited for: 1 -> 0; matrix products, arithmetic and copies ran while one was open for 1% -> 0% of each run, Pallas kernels for 0% -> 0%
where the time goes in v1:
time: 288 us
  Pallas kernels  265 us (92%)
  matrix products  9.1 us (3%)
  other arithmetic  8.49 us (3%)
  local copies, waits for them, and re-layouts  4.18 us (1%)
    pallas_call x1, Pallas kernels, channelize(): pl.pallas_call(functools.partial(channelize_kernel, points, tap_count, fr...  222 us
    pallas_call x1, Pallas kernels, exchange(): pl.pallas_call(functools.partial(exchange_kernel, count, sec_count), out_...  30 us
    pallas_call x1, Pallas kernels, total_power(): pl.pallas_call(functools.partial(power_kernel, count, sec_count), out_sha...  12.9 us

profile of v1, /device:TPU:15, one launch (start us, length us, event | category | flops | bytes accessed | tf_op | source)
XLA Modules:
  0.0 287.5 jit_solution(8915409938070212483)
XLA Ops:
  0.6 0.8 maximum_bitcast_fusion.2.gain_ref
  1.4 0.7 pad_add_fusion
  2.2 0.9 multiply_bitcast_fusion.1
  3.1 0.0 copy-start.1
  3.1 4.0 %fusion.1 = bf16[16,1,512]{2,1,0:T(2,128)(2,1)S(1)} fusion(s32[16,512]{1,0:T(8,128)} %param.14, bf16[16,512,1]{1,0,2:T(8,128)(2,1)S(1)} %get-tuple-element.16), kind=kOutput, calls=%fused_computation.2 | convolution fusion | flops 12582912 | bytes 65536 | tf_op jit(solution)/shard_map/bk,bks->bs/dot_general | solution.py:32
  7.1 0.0 copy-done.1
  7.1 0.0 copy-start
  7.2 3.2 %fusion = bf16[16,1,512]{2,1,0:T(2,128)(2,1)S(1)} fusion(s32[16,512]{1,0:T(8,128)S(1)} %copy-done.1, bf16[16,512,1]{1,0,2:T(8,128)(2,1)S(1)} %get-tuple-element.17), kind=kOutput, calls=%fused_computation.1 | convolution fusion | flops 12582912 | bytes 65536 | tf_op jit(solution)/shard_map/bk,bks->bs/dot_general | solution.py:33
  10.4 0.3 fusion.35
  10.7 0.0 copy-done
  10.7 0.2 broadcast_in_dim.6.taps_ref
  10.9 0.7 multiply_convert_fusion.2
  11.6 0.2 bitcast_negate_fusion
  11.8 1.2 maximum_bitcast_fusion
  13.0 0.2 pad_maximum_fusion.1.table_ref
  13.2 222.0 %channelize.1 = bf16[64,8192]{1,0:T(8,128)(2,1)S(1)} custom-call(bf16[2,32,569344]{2,1,0:T(8,128)(2,1)} %volt_ref.1, bf16[12,16,4096]{2,1,0:T(8,128)(2,1)S(1)} %broadcast_in_dim.6.taps_ref, bf16[2,4096,128]{2,1,0:T(8,128)(2,1)S(1)} %pad_maximum_fusion.1.table_ref, f32[1,128]{1,0:T(1,128)S(1)} %maximum_bitcast_fusion.2.gain_ref), custom_call_target="tpu_custom_call" | custom-call | tf_op jit(solution)/shard_map/channelize/pallas_call | solution.py:233
  235.2 1.2 copy.20
  236.4 30.0 %exchange.1 = bf16[2,32,32,256]{3,2,1,0:T(8,128)(2,1)} custom-call(bf16[2,32,32,256]{3,2,1,0:T(8,128)(2,1)} %bitcast.56), custom_call_target="tpu_custom_call" | custom-call | tf_op jit(solution)/shard_map/exchange/pallas_call | solution.py:301
  266.5 1.3 fusion.37
  267.7 0.2 reshape.269
  267.9 0.2 convolution_bitcast_fusion.1
  268.1 0.2 convolution_bitcast_fusion
  268.3 0.1 multiply_reduce_fusion
  268.4 0.7 broadcast_in_dim.8.x_ref
  269.1 12.9 %power.1 = f32[16,128]{1,0:T(8,128)} custom-call(f32[16,128]{1,0:T(8,128)} %broadcast_in_dim.8.x_ref), custom_call_target="tpu_custom_call" | custom-call | tf_op jit(solution)/shard_map/power/pallas_call | solution.py:347
  282.0 0.8 rsqrt_reduce_fusion
  282.9 0.1 multiply_convert_fusion.4
  282.9 0.6 copy.15
  283.6 0.1 fusion.38
  283.6 0.7 fusion.5
  284.4 0.7 fusion.4
  285.1 2.4 pad_maximum_fusion
  (2 shorter events, 0.0 us)
Async XLA Ops:
  3.1 4.0 %copy-start.1 = (s32[16,512]{1,0:T(8,128)S(1)}, s32[16,512]{1,0:T(8,128)}, u32[]{:S(2)}) copy-start(s32[16,512]{1,0:T(8,128)} %param.14) | copy-start | bytes 98308
  7.1 3.5 %copy-start = (f32[12,4096]{1,0:T(8,128)S(1)}, f32[12,4096]{1,0:T(8,128)}, u32[]{:S(2)}) copy-start(f32[12,4096]{1,0:T(8,128)} %param.9) | copy-start | bytes 589828

commit v2 on v1

--- a/solution.py
+++ b/solution.py
@@ -113,7 +113,7 @@
 
 MESH = pl.DeviceIdType.MESH
 ROWS = 16
-CHUNK = 512
+CHUNK = 1024
 STEP = 256
 
 
@@ -140,15 +140,6 @@
     )
 
 
-def tree_sum(terms):
-    while len(terms) > 1:
-        paired = [terms[k] + terms[k + 1] for k in range(0, len(terms) - 1, 2)]
-        if len(terms) % 2:
-            paired.append(terms[-1])
-        terms = paired
-    return terms[0]
-
-
 def channelize_kernel(
     points, tap_count, frames, groups, volt_ref, taps_ref, table_ref, gain_ref, out_ref,
     held, filtered, total, sem,
@@ -195,10 +186,21 @@
             lanes = pl.ds(here, 128)
             point = pl.ds(pl.multiple_of(chunk * CHUNK + here, 128), 128)
             taps = [taps_ref[t, :, point] for t in range(tap_count)]
-            window = [held[slot, t, part, :, lanes] for t in range(tap_count - 1)]
+
+            def load(frame):
+                wide = held[slot, frame, part, :, lanes].astype(jnp.float32)
+                return wide[:8], wide[8:]
+
+            window = [load(t) for t in range(tap_count - 1)]
             for s in range(spectra):
-                window.append(held[slot, s + tap_count - 1, part, :, lanes])
-                value = tree_sum([tap * frame for tap, frame in zip(taps, window)])
+                window.append(load(s + tap_count - 1))
+                halves = []
+                for half in range(2):
+                    value = taps[0] * window[0][half]
+                    for t in range(1, tap_count):
+                        value = value + taps[t] * window[t][half]
+                    halves.append(value)
+                value = jnp.concatenate(halves, axis=0).astype(jnp.bfloat16)
                 filtered[s * ROWS : (s + 1) * ROWS, tile * 128 : (tile + 1) * 128] = value
                 window = window[1:]
         span = pl.ds(pl.multiple_of(chunk * CHUNK + piece * STEP, STEP), STEP)
@@ -226,7 +228,7 @@
     spectra = frames - tap_count + 1
     slots = slot_gain.shape[0]
     groups = inputs_here // ROWS
-    taps = jnp.broadcast_to(fir_taps.astype(jnp.bfloat16)[:, None, :], (tap_count, ROWS, points))
+    taps = jnp.broadcast_to(fir_taps[:, None, :], (tap_count, 8, points))
     gain = jnp.concatenate([slot_gain, slot_gain])[None, :]
     whole = pl.BlockSpec(memory_space=pltpu.VMEM)
     width = ROWS * 2 * spectra

time: 288 us -> 234 us (0.81)
  Pallas kernels: 265 us -> 211 us
    pallas_call x1, Pallas kernels: 222 us -> 168 us  [channelize(): pl.pallas_call(functools.partial(channelize_kernel, points, tap_count, fr...]
where the time goes in v2:
time: 234 us; the launch traced here: 233 us
  Pallas kernels  211 us (90%)
  matrix products  9.1 us (4%)
  other arithmetic  8.47 us (4%)
  local copies, waits for them, and re-layouts  4.15 us (2%)
    pallas_call x1, Pallas kernels, channelize(): pl.pallas_call(functools.partial(channelize_kernel, points, tap_count, fr...  168 us
    pallas_call x1, Pallas kernels, exchange(): pl.pallas_call(functools.partial(exchange_kernel, count, sec_count), out_...  30 us
    pallas_call x1, Pallas kernels, total_power(): pl.pallas_call(functools.partial(power_kernel, count, sec_count), out_sha...  12.9 us

profile of v2, /device:TPU:15, one launch (start us, length us, event | category | flops | bytes accessed | tf_op | source)
XLA Modules:
  0.0 233.3 jit_solution(5737086584650837447)
XLA Ops:
  0.6 0.8 maximum_bitcast_fusion.2.gain_ref
  1.4 0.7 pad_add_fusion
  2.2 0.9 multiply_bitcast_fusion.1
  3.1 0.0 copy-start.1
  3.1 4.0 %fusion.1 = bf16[16,1,512]{2,1,0:T(2,128)(2,1)S(1)} fusion(s32[16,512]{1,0:T(8,128)} %param.14, bf16[16,512,1]{1,0,2:T(8,128)(2,1)S(1)} %get-tuple-element.16), kind=kOutput, calls=%fused_computation.2 | convolution fusion | flops 12582912 | bytes 65536 | tf_op jit(solution)/shard_map/bk,bks->bs/dot_general | solution.py:32
  7.1 0.0 copy-done.1
  7.1 0.0 copy-start
  7.2 3.2 %fusion = bf16[16,1,512]{2,1,0:T(2,128)(2,1)S(1)} fusion(s32[16,512]{1,0:T(8,128)S(1)} %copy-done.1, bf16[16,512,1]{1,0,2:T(8,128)(2,1)S(1)} %get-tuple-element.17), kind=kOutput, calls=%fused_computation.1 | convolution fusion | flops 12582912 | bytes 65536 | tf_op jit(solution)/shard_map/bk,bks->bs/dot_general | solution.py:33
  10.4 0.3 fusion.35
  10.7 0.0 copy-done
  10.7 0.1 broadcast_in_dim.6.taps_ref
  10.8 0.7 multiply_convert_fusion.2
  11.5 0.2 bitcast_negate_fusion
  11.7 1.2 maximum_bitcast_fusion
  12.9 0.2 pad_maximum_fusion.1.table_ref
  13.1 167.9 %channelize.1 = bf16[64,8192]{1,0:T(8,128)(2,1)S(1)} custom-call(bf16[2,32,569344]{2,1,0:T(8,128)(2,1)} %volt_ref.1, f32[12,8,4096]{2,1,0:T(8,128)S(1)} %broadcast_in_dim.6.taps_ref, bf16[2,4096,128]{2,1,0:T(8,128)(2,1)S(1)} %pad_maximum_fusion.1.table_ref, f32[1,128]{1,0:T(1,128)S(1)} %maximum_bitcast_fusion.2.gain_ref), custom_call_target="tpu_custom_call" | custom-call | tf_op jit(solution)/shard_map/channelize/pallas_call | solution.py:235
  181.0 1.2 copy.20
  182.2 30.0 %exchange.1 = bf16[2,32,32,256]{3,2,1,0:T(8,128)(2,1)} custom-call(bf16[2,32,32,256]{3,2,1,0:T(8,128)(2,1)} %bitcast.56), custom_call_target="tpu_custom_call" | custom-call | tf_op jit(solution)/shard_map/exchange/pallas_call | solution.py:303
  212.3 1.3 fusion.37
  213.5 0.2 reshape.269
  213.7 0.2 convolution_bitcast_fusion.1
  213.9 0.2 convolution_bitcast_fusion
  214.1 0.1 multiply_reduce_fusion
  214.2 0.7 broadcast_in_dim.8.x_ref
  214.9 12.9 %power.1 = f32[16,128]{1,0:T(8,128)} custom-call(f32[16,128]{1,0:T(8,128)} %broadcast_in_dim.8.x_ref), custom_call_target="tpu_custom_call" | custom-call | tf_op jit(solution)/shard_map/power/pallas_call | solution.py:349
  227.8 0.8 rsqrt_reduce_fusion
  228.7 0.1 multiply_convert_fusion.4
  228.7 0.6 copy.15
  229.4 0.1 fusion.38
  229.4 0.7 fusion.5
  230.2 0.7 fusion.4
  230.9 2.4 %pad_maximum_fusion = bf16[1,2,1024,1024]{3,2,1,0:T(8,128)(2,1)} fusion(bf16[1,1,1024,1024]{3,2,1,0:T(8,128)(2,1)S(1)} %fusion.5, bf16[1,1,1024,1024]{3,2,1,0:T(8,128)(2,1)S(1)} %fusion.4), kind=kLoop, calls=%fused_computation.5 | loop fusion | flops 2097152 | bytes 8388608 | tf_op jit(solution)/shard_map/stack | solution.py:397
  (1 shorter events, 0.0 us)
Async XLA Ops:
  3.1 4.0 %copy-start.1 = (s32[16,512]{1,0:T(8,128)S(1)}, s32[16,512]{1,0:T(8,128)}, u32[]{:S(2)}) copy-start(s32[16,512]{1,0:T(8,128)} %param.14) | copy-start | bytes 98308
  7.1 3.5 %copy-start = (f32[12,4096]{1,0:T(8,128)S(1)}, f32[12,4096]{1,0:T(8,128)}, u32[]{:S(2)}) copy-start(f32[12,4096]{1,0:T(8,128)} %param.9) | copy-start | bytes 589828
